TPU v7x, 32 devices: a whole 2x2x4 slice. The times are simulated.
32 devices in a mesh: dp: 8 (over z, y), seq: 4 (over x, core).
Axes of the slice: x: 2, y: 2, z: 4, core: 2. Of those that a mesh axis runs over, the one named last changes fastest.
Arguments:
- slot_tokens: bfloat16 [104, 256, 1152], P('dp', 'seq'), may hold values from -12 to 12
- modulation: float32 [8, 6, 1152], P('dp'), may hold values from -2.5 to 2.5
- counts: int32 [8], replicated, may hold values from 1 to 13, as said below
- dest: int32 [8, 13], replicated, may hold values from 0 to 55, as said below
- qkv_spatial: bfloat16 [1152, 1728], replicated, may hold values from -4 to 4
- out_spatial: bfloat16 [576, 1152], replicated, may hold values from -0.25 to 0.25
- qkv_temporal: bfloat16 [1152, 1728], replicated, may hold values from -4 to 4
- out_temporal: bfloat16 [576, 1152], replicated, may hold values from -0.25 to 0.25
Outputs:
- video_out: bfloat16 [56, 256, 1152], P('dp', 'seq')
Inputs may be any that keep to these rules, and one draw needn't show every extreme that they name: Group g holds blocks in slots 0 to counts[g] - 1; the counts sum to 56; some group holds 13 blocks. Over the slots q below counts[g] of all groups g, dest[g, q] takes every value 0 to 55 exactly once; one group sends at most 2 blocks to one video, and some group sends 2; entries at slots from counts[g] on are arbitrary values of the same range.
All inputs are finite; a program needn't handle non-finite values.
Results may differ from a plain program's by a relative error of at most 0.0057.
Values may be sent and summed in bfloat16 or wider, within the bound.
A program may use at most 64 MiB of HBM per device.

v0:
```python
import math

import jax
import jax.numpy as jnp
from jax import lax
from jax.sharding import PartitionSpec as P

HEADS = 8
HEAD_DIM = 72
NFD = 7


epsilon = 1e-06


def norm_mod(tokens, shift_row, scale_row):
    values = tokens.astype(jnp.float32)
    center = values - jnp.mean(values, axis=-1, keepdims=True)
    spread = jnp.mean(center * center, axis=-1, keepdims=True)
    return (center * lax.rsqrt(spread + epsilon) * (1.0 + scale_row) + shift_row).astype(
        jnp.bfloat16
    )


def attention(qkv_rows, batch_count, length):
    parts = qkv_rows.reshape(batch_count, length, 3, HEADS, HEAD_DIM)
    factor = 1.0 / math.sqrt(HEAD_DIM)
    scores = (
        jnp.einsum(
            "bqhs,bkhs->bhqk", parts[:, :, 0], parts[:, :, 1], preferred_element_type=jnp.float32
        )
        * factor
    )
    highest = jnp.max(scores, axis=-1, keepdims=True)
    raised = jnp.exp(scores - highest)
    weights = (raised / jnp.sum(raised, axis=-1, keepdims=True)).astype(jnp.bfloat16)
    mixed = jnp.einsum(
        "bhqk,bkhs->bqhs", weights, parts[:, :, 2], preferred_element_type=jnp.float32
    )
    return mixed.astype(jnp.bfloat16).reshape(batch_count * length, HEADS * HEAD_DIM)


def spatial_block(frames, modulation_rows, w_qkv, w_out):
    frame_count, patch_count, model_width = frames.shape
    shift_rows = modulation_rows[:, 0][:, None, :]
    scale_rows = modulation_rows[:, 1][:, None, :]
    gate_rows = modulation_rows[:, 2][:, None, :]
    normed = norm_mod(frames, shift_rows, scale_rows)
    qkv_rows = jnp.dot(
        normed.reshape(-1, model_width), w_qkv, preferred_element_type=jnp.float32
    ).astype(jnp.bfloat16)
    mixed = attention(qkv_rows, frame_count, patch_count)
    projected = jnp.dot(mixed, w_out, preferred_element_type=jnp.float32).reshape(
        frame_count, patch_count, model_width
    )
    return (frames.astype(jnp.float32) + gate_rows * projected).astype(jnp.bfloat16)


def on_device(
    slot_tokens, modulation, counts, dest, qkv_spatial, out_spatial, qkv_temporal, out_temporal
):
    group_count = lax.axis_size("dp")
    slot_count, patch_count, model_width = slot_tokens.shape
    block_count = NFD
    send_room = (slot_count + group_count - 1) // group_count
    group_index = lax.axis_index("dp")
    slot_ids = jnp.arange(slot_count, dtype=jnp.int32)
    group_ids = jnp.arange(group_count, dtype=jnp.int32)
    room_ids = jnp.arange(send_room, dtype=jnp.int32)
    live_slots = slot_ids[None, :] < counts[:, None]
    target_group = dest // block_count
    earlier = slot_ids[:, None] < slot_ids[None, :]
    same_target = (
        live_slots[:, :, None]
        & (target_group[:, :, None] == target_group[:, None, :])
        & earlier[None, :, :]
    )
    send_rank = jnp.sum(same_target.astype(jnp.int32), axis=1)
    own_live = lax.dynamic_index_in_dim(
        live_slots.astype(jnp.int32), group_index, 0, keepdims=False
    )
    own_target = lax.dynamic_index_in_dim(target_group, group_index, 0, keepdims=False)
    own_rank = lax.dynamic_index_in_dim(send_rank, group_index, 0, keepdims=False)
    picks = (
        (own_live[:, None, None] > 0)
        & (own_target[:, None, None] == group_ids[None, :, None])
        & (own_rank[:, None, None] == room_ids[None, None, :])
    )
    chosen_slot = jnp.sum(picks.astype(jnp.int32) * slot_ids[:, None, None], axis=0).reshape(-1)
    payload = jnp.take(slot_tokens, chosen_slot, axis=0)
    arrived = lax.all_to_all(payload, "dp", split_axis=0, concat_axis=0, tiled=True)
    wanted = group_index * block_count + jnp.arange(block_count, dtype=jnp.int32)
    matches = (live_slots[:, :, None] & (dest[:, :, None] == wanted[None, None, :])).astype(
        jnp.int32
    )
    source_group = jnp.sum(matches * group_ids[:, None, None], axis=(0, 1))
    source_rank = jnp.sum(matches * send_rank[:, :, None], axis=(0, 1))
    placed = jnp.take(arrived, source_group * send_room + source_rank, axis=0)
    local_frames = spatial_block(placed, modulation, qkv_spatial, out_spatial)
    own_modulation = modulation[0]
    shard_count = lax.axis_size("seq")
    widest = patch_count // shard_count
    frame_total = shard_count * block_count
    channels = local_frames.shape[-1]
    selected = local_frames.reshape(block_count, shard_count, widest, channels)
    moved = lax.all_to_all(selected, "seq", split_axis=1, concat_axis=0, tiled=True)
    token_rows = moved.reshape(frame_total * widest, channels)
    normed_rows = norm_mod(token_rows, own_modulation[3], own_modulation[4])
    qkv_rows = jnp.dot(normed_rows, qkv_temporal, preferred_element_type=jnp.float32).astype(
        jnp.bfloat16
    )
    qkv_width = qkv_rows.shape[-1]
    by_patch = (
        qkv_rows.reshape(frame_total, widest, qkv_width)
        .transpose(1, 0, 2)
        .reshape(widest * frame_total, qkv_width)
    )
    mixed = attention(by_patch, widest, frame_total)
    attn_width = mixed.shape[-1]
    mixed = (
        mixed.reshape(widest, frame_total, attn_width)
        .transpose(1, 0, 2)
        .reshape(frame_total * widest, attn_width)
    )
    projected_rows = jnp.dot(mixed, out_temporal, preferred_element_type=jnp.float32)
    homeward = (token_rows.astype(jnp.float32) + own_modulation[5] * projected_rows).astype(
        jnp.bfloat16
    )
    back_width = homeward.shape[-1]
    returned = lax.all_to_all(
        homeward.reshape(frame_total, 1, widest, back_width),
        "seq",
        split_axis=0,
        concat_axis=1,
        tiled=True,
    )
    restored = returned.reshape(block_count, patch_count, back_width)
    return restored


def solution(mesh):
    in_specs = (P("dp", "seq", None), P("dp", None, None), P(), P(), P(), P(), P(), P())
    out_specs = P("dp", "seq", None)
    return jax.shard_map(
        on_device, mesh=mesh, in_specs=in_specs, out_specs=out_specs, check_vma=False
    )
```

profile of v0, /device:TPU:0, one launch (start us, length us, event | category | flops | bytes accessed | tf_op | source)
XLA Modules:
  0.0 166.1 jit_solution(7982996874267889492)
XLA Ops:
  2.4 2.2 %gather_fusion = bf16[16,64,1152]{2,1,0:T(8,128)(2,1)} fusion(bf16[13,64,1152]{2,1,0:T(8,128)(2,1)S(1)} %copy-done, s32[1024]{0:T(1024)S(1)} %pad_clamp_fusion.1), kind=kCustom, calls=%fused_computation | custom fusion | bytes 4718656 | tf_op jit(solution)/shard_map/jit(_take)/gather | solution.py:90
  4.6 3.4 %broadcast_select_fusion = bf16[16,64,1152]{2,1,0:T(8,128)(2,1)} fusion(bf16[16,64,1152]{2,1,0:T(8,128)(2,1)} %gather_fusion, pred[16]{0:T(512)(128)(4,1)S(1)} %compare_and_fusion.1), kind=kLoop, calls=%fused_computation.14 | loop fusion | flops 1179648 | bytes 4718608 | tf_op jit(solution)/shard_map/jit(_take)/select_n | solution.py:90
  7.9 7.4 %all-to-all-start = ((bf16[16,64,1152]{2,1,0:T(8,128)(2,1)}), bf16[16,64,1152]{2,1,0:T(8,128)(2,1)}, u32[]{:S(2)}, u32[]{:S(2)}) async-start(bf16[16,64,1152]{2,1,0:T(8,128)(2,1)} %broadcast_select_fusion), calls=%async_computation | async-start | bytes 4718592 | tf_op jit(solution)/shard_map/all_to_all | solution.py:91
  16.1 53.2 %all-to-all-done = bf16[16,64,1152]{2,1,0:T(8,128)(2,1)} async-done(((bf16[16,64,1152]{2,1,0:T(8,128)(2,1)}), bf16[16,64,1152]{2,1,0:T(8,128)(2,1)}, u32[]{:S(2)}, u32[]{:S(2)}) %all-to-all-start) | async-done | bytes 2359328 | tf_op jit(solution)/shard_map/all_to_all | solution.py:91
  69.3 2.4 %gather_fusion.1 = bf16[7,64,1152]{2,1,0:T(8,128)(2,1)S(1)} fusion(bf16[16,64,1152]{2,1,0:T(8,128)(2,1)} %all-to-all-done, s32[1024]{0:T(1024)S(1)} %pad_clamp_fusion), kind=kCustom, calls=%fused_computation.1 | custom fusion | bytes 2064412 | tf_op jit(solution)/shard_map/jit(_take)/gather | solution.py:98
  72.9 5.7 %convolution_convert_fusion.1 = bf16[448,1728]{1,0:T(8,128)(2,1)} fusion(bf16[1152,1728]{0,1:T(8,128)(2,1)} %param.12, bf16[448,1152]{1,0:T(8,128)(2,1)S(1)} %bitcast_select_fusion, f32[1152]{0:T(1024)S(1)} %get-tuple-element.6, f32[1152]{0:T(1024)S(1)} %get-tuple-element.7, f32[448]{0:T(512)S(1)} %rsqrt.23, f32[448]{0:T(512)S(1)} %div.40), kind=kOutput, calls=%fused_computation.11 | convolution fusion | flops 1787498496 | bytes 6574592 | tf_op jit(solution)/shard_map/dot_general | solution.py:49
  78.7 5.4 %reshape.310 = bf16[7,64,3,8,72]{4,3,2,1,0:T(8,128)(2,1)} reshape(bf16[448,1728]{1,0:T(8,128)(2,1)} %convolution_convert_fusion.1) | data formatting | bytes 3096576 | tf_op jit(solution)/shard_map/reshape | solution.py:26
  84.1 2.9 %fusion.46 = (bf16[7,64,1,8,72]{4,3,2,1,0:T(8,128)(2,1)S(1)}, bf16[7,64,1,8,72]{4,3,2,1,0:T(8,128)(2,1)}, bf16[7,64,1,8,72]{4,3,2,1,0:T(8,128)(2,1)S(1)}) fusion(bf16[7,64,3,8,72]{4,3,2,1,0:T(8,128)(2,1)} %reshape.310), kind=kLoop, calls=%fused_computation.107 | loop fusion | bytes 3096576 | tf_op jit(solution)/shard_map/slice | solution.py:30
  88.2 1.9 %fusion.26 = f32[7,8,64,64]{2,3,1,0:T(8,128)} fusion(bf16[7,64,1,8,72]{4,3,2,1,0:T(8,128)(2,1)S(1)} %get-tuple-element.18, bf16[7,64,1,8,72]{4,3,2,1,0:T(8,128)(2,1)S(1)} %get-tuple-element.16), kind=kOutput, calls=%fused_computation.54 | convolution fusion | flops 33030144 | bytes 1949696 | tf_op jit(solution)/shard_map/bqhs,bkhs->bhqk/dot_general | solution.py:29
  90.0 2.3 %fusion.47 = f32[7,8,64]{2,1,0:T(8,128)S(1)} fusion(bf16[7,64,1,8,72]{4,3,2,1,0:T(8,128)(2,1)} %copy-done.2, bf16[7,64,1,8,72]{4,3,2,1,0:T(8,128)(2,1)} %copy-done.1), kind=kOutput, calls=%fused_computation.108 | convolution fusion | flops 33718336 | bytes 1046528 | tf_op jit(solution)/shard_map/sub | solution.py:35
  92.4 3.5 %fusion.17 = bf16[7,64,8,72]{3,1,2,0:T(8,128)(2,1)} fusion(bf16[7,64,1,8,72]{4,3,2,1,0:T(8,128)(2,1)} %get-tuple-element.17, f32[7,8,64]{2,1,0:T(8,128)S(1)} %fusion.47, f32[7,8,64,64]{2,3,1,0:T(8,128)} %fusion.26), kind=kOutput, calls=%fused_computation.38 | convolution fusion | flops 34209344 | bytes 1964032 | tf_op jit(solution)/shard_map/bhqk,bkhs->bqhs/dot_general | solution.py:37
  95.9 2.7 %copy.55 = bf16[7,64,8,72]{3,2,1,0:T(8,128)(2,1)} copy(bf16[7,64,8,72]{3,1,2,0:T(8,128)(2,1)} %fusion.17) | data formatting | bytes 1032192 | tf_op jit(solution)/shard_map/convert_element_type | solution.py:40
  98.6 1.9 %dot_general.29 = bf16[7,64,576]{2,1,0:T(8,128)(2,1)S(1)} reshape(bf16[7,64,8,72]{3,2,1,0:T(8,128)(2,1)} %copy.55) | data formatting | bytes 1032192 | tf_op jit(solution)/shard_map/dot_general | solution.py:53
  100.5 2.4 %fusion.5 = bf16[7,64,1152]{2,1,0:T(8,128)(2,1)S(1)} fusion(bf16[7,64,576]{2,1,0:T(8,128)(2,1)S(1)} %dot_general.29, bf16[576,1152]{1,0:T(8,128)(2,1)} %param.13, f32[1152]{0:T(1024)S(1)} %get-tuple-element.8, bf16[7,64,1152]{2,1,0:T(8,128)(2,1)S(1)} %gather_fusion.1, pred[7]{0:T(512)(128)(4,1)} %copy-done.6), kind=kOutput, calls=%fused_computation.13 | convolution fusion | flops 597123072 | bytes 3912199 | tf_op jit(solution)/shard_map/dot_general | solution.py:53
  103.0 16.8 %all_to_all.29 = bf16[7,4,16,1152]{3,2,0,1:T(8,128)(2,1)S(1)} all-to-all(bf16[7,4,16,1152]{3,2,0,1:T(8,128)(2,1)S(1)} %copy.56), channel_id=1, replica_groups=mesh['dp'=8,'seq'=4] {'seq'}, dimensions={1} | all-to-all | bytes 2064384 | tf_op jit(solution)/shard_map/all_to_all | solution.py:106
  121.1 5.6 %convolution_convert_fusion = bf16[448,1728]{1,0:T(8,128)(2,1)} fusion(bf16[448,1152]{1,0:T(8,128)(2,1)S(1)} %fusion.11, bf16[1152,1728]{0,1:T(8,128)(2,1)} %param.14), kind=kOutput, calls=%fused_computation.10 | convolution fusion | flops 1784401920 | bytes 6561792 | tf_op jit(solution)/shard_map/dot_general | solution.py:109
  126.7 5.4 %reshape_reshape.6 = bf16[16,28,3,8,72]{4,3,2,0,1:T(8,128)(2,1)} reshape(bf16[16,28,1728]{2,0,1:T(8,128)(2,1)} %bitcast.123) | data formatting | bytes 3096576 | tf_op jit(solution)/shard_map/reshape;reshape | solution.py:26
  132.1 3.4 %fusion.45 = (bf16[16,28,1,8,72]{4,3,2,0,1:T(8,128)(2,1)}, bf16[16,28,1,8,72]{4,3,2,0,1:T(8,128)(2,1)}, bf16[16,28,1,8,72]{4,3,2,0,1:T(8,128)(2,1)}) fusion(bf16[16,28,3,8,72]{4,3,2,0,1:T(8,128)(2,1)} %reshape_reshape.6), kind=kLoop, calls=%fused_computation.106 | loop fusion | bytes 3096576 | tf_op jit(solution)/shard_map/slice | solution.py:38
  135.4 4.6 %fusion.48 = (f32[16,8,28]{2,1,0:T(8,128)S(1)}, f32[16,8,28,28]{2,3,1,0:T(8,128)}) fusion(bf16[16,28,1,8,72]{4,3,2,0,1:T(8,128)(2,1)} %get-tuple-element.15, bf16[16,28,1,8,72]{4,3,2,0,1:T(8,128)(2,1)} %get-tuple-element.14), kind=kOutput, calls=%fused_computation.109 | convolution fusion | flops 14751771 | bytes 1447936 | tf_op jit(solution)/shard_map/sub | solution.py:35
  140.0 2.7 %fusion.16 = bf16[16,28,8,72]{3,1,2,0:T(8,128)(2,1)S(1)} fusion(f32[16,8,28,28]{2,3,1,0:T(8,128)} %get-tuple-element.22, bf16[16,28,1,8,72]{4,3,2,0,1:T(8,128)(2,1)} %get-tuple-element.13, f32[16,8,28]{2,1,0:T(8,128)S(1)} %get-tuple-element.21), kind=kOutput, calls=%fused_computation.37 | convolution fusion | flops 14909440 | bytes 1447936 | tf_op jit(solution)/shard_map/bhqk,bkhs->bqhs/dot_general | solution.py:37
  142.7 1.3 copy.66
  144.0 1.9 %reshape_reshape.7 = bf16[16,28,576]{2,0,1:T(8,128)(2,1)S(1)} reshape(bf16[16,28,8,72]{3,2,0,1:T(8,128)(2,1)} %copy.66) | data formatting | bytes 1032192 | tf_op jit(solution)/shard_map/reshape;reshape | solution.py:121
  146.1 1.2 copy-done.3
  148.4 16.7 %all_to_all.30 = bf16[28,1,16,1152]{3,2,1,0:T(8,128)(2,1)S(1)} all-to-all(bf16[28,1,16,1152]{3,2,1,0:T(8,128)(2,1)S(1)} %bitcast.120), channel_id=1, replica_groups=mesh['dp'=8,'seq'=4] {'seq'}, dimensions={0} | all-to-all | bytes 2064384 | tf_op jit(solution)/shard_map/all_to_all | solution.py:130
  (56 shorter events, 9.0 us)
Async XLA Ops:
  0.0 2.4 %copy-start = (bf16[13,64,1152]{2,1,0:T(8,128)(2,1)S(1)}, bf16[13,64,1152]{2,1,0:T(8,128)(2,1)}, u32[]{:S(2)}) copy-start(bf16[13,64,1152]{2,1,0:T(8,128)(2,1)} %param.8) | copy-start | bytes 5750788
  7.9 7.4 %copy-start.5 = (s32[8,13]{1,0:T(8,128)S(1)}, s32[8,13]{1,0:T(8,128)}, u32[]{:S(2)}) copy-start(s32[8,13]{1,0:T(8,128)} %param.11) | copy-start | bytes 1252
  7.9 8.1 %copy-start.4 = (f32[1,6,1152]{2,0,1:T(1,128)S(1)}, f32[1,6,1152]{2,0,1:T(1,128)}, u32[]{:S(2)}) copy-start(f32[1,6,1152]{2,0,1:T(1,128)} %param.9) | copy-start | bytes 82948
  7.9 61.4 %all-to-all-start = ((bf16[16,64,1152]{2,1,0:T(8,128)(2,1)}), bf16[16,64,1152]{2,1,0:T(8,128)(2,1)}, u32[]{:S(2)}, u32[]{:S(2)}) async-start(bf16[16,64,1152]{2,1,0:T(8,128)(2,1)} %broadcast_select_fusion), calls=%async_computation | async-start | bytes 4718592 | tf_op jit(solution)/shard_map/all_to_all | solution.py:91
  15.8 56.7 %copy-start.6 = (pred[7]{0:T(512)(128)(4,1)}, pred[7]{0:T(512)(128)(4,1)S(1)}, u32[]{:S(2)}) copy-start(pred[7]{0:T(512)(128)(4,1)S(1)} %compare_and_fusion.2) | copy-start | bytes 25
  87.0 0.9 copy-start.1
  87.0 1.2 copy-start.2
  145.9 1.3 copy-start.3
where the time goes:
time: 167 us; the launch traced here: 166 us
  waiting for transfers between devices  53.2 us (32%)
  local copies, waits for them, and re-layouts  33.9 us (20%)
  blocking collectives  33.6 us (20%)
  matrix products  29.8 us (18%)
  other arithmetic  8.02 us (5%)
  starting transfers between devices  7.42 us (4%)
    all_to_all x1, waiting for transfers between devices, on_device(): lax.all_to_all(payload, 'dp', split_axis=0, concat_axis=0, tiled=True)  53.2 us
    all_to_all x1, blocking collectives, on_device(): lax.all_to_all(selected, 'seq', split_axis=1, concat_axis=0, tiled=True)  16.8 us
    all_to_all x1, blocking collectives, on_device(): lax.all_to_all(homeward.reshape(frame_total, 1, widest, back_width), 'seq...  16.7 us
    all_to_all x1, starting transfers between devices, on_device(): lax.all_to_all(payload, 'dp', split_axis=0, concat_axis=0, tiled=True)  7.42 us
    sub x2, matrix products, attention(): raised = jnp.exp(scores - highest)  6.89 us
    dot_general x2, matrix products, attention(): jnp.einsum('bhqk,bkhs->bqhs', weights, parts[:, :, 2], preferred_element_...  6.24 us
    dot_general x1, matrix products, spatial_block(): jnp.dot(normed.reshape(-1, model_width), w_qkv, preferred_element_type=jn...  5.75 us
    dot_general x1, matrix products, on_device(): jnp.dot(normed_rows, qkv_temporal, preferred_element_type=jnp.float32)  5.57 us
  transfers between devices with their start and end apart: 1, of which 1 were waited for; matrix products, arithmetic and copies ran while one was open for 0% of the time, Pallas kernels for 0%

commit v1 on v0

v1 whole, which is shorter than its diff:
```python
import functools
import math

import jax
import jax.numpy as jnp
from jax import lax
from jax.experimental import pallas as pl
from jax.experimental.pallas import tpu as pltpu
from jax.sharding import PartitionSpec as P

HEADS = 8
HEAD_DIM = 72
NFD = 7
EPSILON = 1e-06
BATCH = 4
HALF = 8
MESH = pl.DeviceIdType.MESH


def norm_mod(values, shift_row, scale_row):
    center = values - jnp.mean(values, axis=-1, keepdims=True)
    spread = jnp.mean(center * center, axis=-1, keepdims=True)
    return (center * lax.rsqrt(spread + EPSILON) * (1.0 + scale_row) + shift_row).astype(jnp.bfloat16)


def attend(qkv, same):
    width = HEADS * HEAD_DIM
    factor = 1.0 / math.sqrt(HEAD_DIM)
    mixed = []
    for head in range(HEADS):
        at = head * HEAD_DIM
        q = qkv[:, at : at + HEAD_DIM]
        k = qkv[:, width + at : width + at + HEAD_DIM]
        v = qkv[:, 2 * width + at : 2 * width + at + HEAD_DIM]
        scores = lax.dot_general(q, k, (((1,), (1,)), ((), ())), preferred_element_type=jnp.float32)
        scores = jnp.where(same, scores * factor, -1e30)
        raised = jnp.exp(scores - jnp.max(scores, axis=-1, keepdims=True))
        weights = (raised * (1.0 / jnp.sum(raised, axis=-1, keepdims=True))).astype(jnp.bfloat16)
        mixed.append(jnp.dot(weights, v, preferred_element_type=jnp.float32))
    return jnp.concatenate(mixed, axis=-1)


def kernel(
    groups, shards, rooms,
    counts_ref, dest_ref, tok_ref, mod_ref, wqs_hbm, wos_hbm, wqt_hbm, wot_hbm,
    out_ref,
    wqs, wos, wqt, wot, send, arr, arr2, rows, res,
    w_sem, dp_send, dp_recv, sq_send, sq_recv, home_send, home_recv,
):
    group = lax.axis_index("dp")
    shard = lax.axis_index("seq")
    slots = tok_ref.shape[0]
    widest, width = tok_ref.shape[2], tok_ref.shape[3]
    patches = shards * widest
    room_slots = rooms * groups
    batches = room_slots // BATCH
    frames = NFD * shards

    barrier = pltpu.get_barrier_semaphore()

    def greet_dp(j, c):
        pl.semaphore_signal(
            barrier, inc=1, device_id=(lax.rem(group + 1 + j, groups), shard), device_id_type=MESH
        )
        return c

    def greet_seq(i, c):
        pl.semaphore_signal(
            barrier, inc=1, device_id=(group, lax.rem(shard + 1 + i, shards)), device_id_type=MESH
        )
        return c

    lax.fori_loop(0, groups - 1, greet_dp, 0)
    lax.fori_loop(0, shards - 1, greet_seq, 0)

    loads = [
        pltpu.make_async_copy(src, dst, w_sem.at[i])
        for i, (src, dst) in enumerate(
            ((wqs_hbm, wqs), (wos_hbm, wos), (wqt_hbm, wqt), (wot_hbm, wot))
        )
    ]
    for load in loads:
        load.start()

    held = counts_ref[group]

    def chosen(target, room):
        pick = jnp.int32(0)
        seen = jnp.int32(0)
        for q in range(slots):
            hit = jnp.logical_and(q < held, dest_ref[group, q] // NFD == target)
            pick = jnp.where(jnp.logical_and(hit, seen == room), jnp.int32(q), pick)
            seen = seen + hit.astype(jnp.int32)
        return pick

    def dp_copy(t):
        target = lax.rem(group + 2 * groups - 1 - lax.rem(t, groups), groups)
        return pltpu.make_async_remote_copy(
            src_ref=send.at[t], dst_ref=arr.at[t],
            send_sem=dp_send.at[t], recv_sem=dp_recv.at[t],
            device_id=(target, shard), device_id_type=MESH,
        )

    def pack(room):
        def body(j, c):
            t = room * groups + j
            target = lax.rem(group + groups - 1 - j, groups)
            send[t] = tok_ref[chosen(target, room)]
            return c
        return body

    def start_dp(room):
        def body(j, c):
            dp_copy(room * groups + j).start()
            return c
        return body

    lax.fori_loop(0, groups, pack(0), 0)
    pl.semaphore_wait(barrier, groups + shards - 2)
    lax.fori_loop(0, groups - 1, start_dp(0), 0)
    for room in range(1, rooms):
        lax.fori_loop(0, groups, pack(room), 0)
        lax.fori_loop(0, groups - 1, start_dp(room), 0)
    for room in range(rooms):
        own = room * groups + groups - 1
        arr[own] = send[own]

    loads[0].wait()
    loads[1].wait()

    def seq_copy(b, i):
        peer = lax.rem(shard + 1 + i, shards)
        return pltpu.make_async_remote_copy(
            src_ref=arr.at[pl.ds(b * BATCH, BATCH), peer],
            dst_ref=arr2.at[shard, pl.ds(b * BATCH, BATCH)],
            send_sem=sq_send.at[b, i], recv_sem=sq_recv.at[b, i],
            device_id=(group, peer), device_id_type=MESH,
        )

    tall = BATCH * patches
    frame_of = lax.broadcasted_iota(jnp.int32, (tall, tall), 0) // patches
    same_frame = frame_of == lax.broadcasted_iota(jnp.int32, (tall, tall), 1) // patches

    def spatial(b, c):
        for n in range(BATCH):
            t = b * BATCH + n

            @pl.when(lax.rem(t, groups) != groups - 1)
            def _():
                dp_copy(t).wait_recv()

        x = arr[pl.ds(b * BATCH, BATCH)].astype(jnp.float32).reshape(tall, width)
        normed = norm_mod(x, mod_ref[0:1, :], mod_ref[1:2, :])
        qkv = jnp.dot(normed, wqs[...], preferred_element_type=jnp.float32).astype(jnp.bfloat16)
        mixed = attend(qkv, same_frame).astype(jnp.bfloat16)
        projected = jnp.dot(mixed, wos[...], preferred_element_type=jnp.float32)
        y = x + mod_ref[2:3, :] * projected
        arr[pl.ds(b * BATCH, BATCH)] = y.reshape(BATCH, shards, widest, width).astype(jnp.bfloat16)
        for i in range(shards - 1):
            seq_copy(b, i).start()
        arr2[shard, pl.ds(b * BATCH, BATCH)] = arr[pl.ds(b * BATCH, BATCH), shard]
        return c

    lax.fori_loop(0, batches, spatial, 0)

    def find(source, found):
        found = list(found)
        live = counts_ref[source]
        seen = jnp.int32(0)
        offset = lax.rem(source + groups - 1 - group + groups, groups)
        for q in range(slots):
            place = dest_ref[source, q] - group * NFD
            hit = jnp.logical_and(q < live, jnp.logical_and(place >= 0, place < NFD))
            code = seen * groups + offset
            for k in range(NFD):
                found[k] = jnp.where(jnp.logical_and(hit, place == k), code, found[k])
            seen = seen + hit.astype(jnp.int32)
        return tuple(found)

    found = lax.fori_loop(0, groups, find, (jnp.int32(0),) * NFD)

    loads[2].wait()
    loads[3].wait()

    def arrived(b, c):
        for i in range(shards - 1):
            seq_copy(b, i).wait_recv()
        return c

    lax.fori_loop(0, batches, arrived, 0)

    for k in range(NFD):
        for s in range(shards):
            rows[k * shards + s] = arr2[s, found[k]]

    halves = widest // HALF
    part = frames * HALF
    x = rows[...].astype(jnp.float32)
    patch_of = lax.rem(lax.broadcasted_iota(jnp.int32, (part, part), 0), HALF)
    same_patch = patch_of == lax.rem(lax.broadcasted_iota(jnp.int32, (part, part), 1), HALF)
    flat = x.reshape(frames * widest, width)
    normed = norm_mod(flat, mod_ref[3:4, :], mod_ref[4:5, :])
    qkv = jnp.dot(normed, wqt[...], preferred_element_type=jnp.float32)
    qkv = qkv.reshape(frames, widest, qkv.shape[-1])
    mixed = []
    for n in range(halves):
        piece = qkv[:, n * HALF : (n + 1) * HALF, :].reshape(part, qkv.shape[-1]).astype(jnp.bfloat16)
        mixed.append(attend(piece, same_patch).reshape(frames, HALF, HEADS * HEAD_DIM))
    mixed = jnp.concatenate(mixed, axis=1).reshape(frames * widest, HEADS * HEAD_DIM).astype(jnp.bfloat16)
    projected = jnp.dot(mixed, wot[...], preferred_element_type=jnp.float32)
    y = (flat + mod_ref[5:6, :] * projected).reshape(frames, widest, width).astype(jnp.bfloat16)
    for k in range(NFD):
        for s in range(shards):
            res[s, k] = y[k * shards + s]

    def home_copy(i):
        peer = lax.rem(shard + 1 + i, shards)
        return pltpu.make_async_remote_copy(
            src_ref=res.at[peer], dst_ref=out_ref.at[:, shard],
            send_sem=home_send.at[i], recv_sem=home_recv.at[i],
            device_id=(group, peer), device_id_type=MESH,
        )

    for i in range(shards - 1):
        home_copy(i).start()
    out_ref[:, shard] = res[shard]

    for room in range(rooms):
        def sent(j, c):
            dp_copy(room * groups + j).wait_send()
            return c
        lax.fori_loop(0, groups - 1, sent, 0)

    def sent_seq(b, c):
        for i in range(shards - 1):
            seq_copy(b, i).wait_send()
        return c

    lax.fori_loop(0, batches, sent_seq, 0)
    for i in range(shards - 1):
        home_copy(i).wait()


def solution(mesh):
    groups, shards = mesh.shape["dp"], mesh.shape["seq"]

    def on_device(tokens, modulation, counts, dest, wqs, wos, wqt, wot):
        slots, patches, width = tokens.shape
        rooms = (slots + groups - 1) // groups
        widest = patches // shards
        total = rooms * groups
        bf = jnp.bfloat16
        vmem = pl.BlockSpec(memory_space=pltpu.VMEM)
        smem = pl.BlockSpec(memory_space=pltpu.SMEM)
        hbm = pl.BlockSpec(memory_space=pl.ANY)
        dma = pltpu.SemaphoreType.DMA
        out = pl.pallas_call(
            functools.partial(kernel, groups, shards, rooms),
            out_shape=jax.ShapeDtypeStruct((NFD, shards, widest, width), bf),
            in_specs=[smem, smem, vmem, vmem, hbm, hbm, hbm, hbm],
            out_specs=vmem,
            scratch_shapes=[
                pltpu.VMEM(wqs.shape, bf),
                pltpu.VMEM(wos.shape, bf),
                pltpu.VMEM(wqt.shape, bf),
                pltpu.VMEM(wot.shape, bf),
                pltpu.VMEM((total, shards, widest, width), bf),
                pltpu.VMEM((total, shards, widest, width), bf),
                pltpu.VMEM((shards, total, widest, width), bf),
                pltpu.VMEM((NFD * shards, widest, width), bf),
                pltpu.VMEM((shards, NFD, widest, width), bf),
                dma((4,)),
                dma((total,)),
                dma((total,)),
                dma((total // BATCH, shards - 1)),
                dma((total // BATCH, shards - 1)),
                dma((shards - 1,)),
                dma((shards - 1,)),
            ],
            compiler_params=pltpu.CompilerParams(
                collective_id=0, has_side_effects=True, vmem_limit_bytes=60 * 1024 * 1024
            ),
        )(counts, dest, tokens.reshape(slots, shards, widest, width), modulation[0], wqs, wos, wqt, wot)
        return out.reshape(NFD, patches, width)

    in_specs = (P("dp", "seq", None), P("dp", None, None), P(), P(), P(), P(), P(), P())
    return jax.shard_map(
        on_device, mesh=mesh, in_specs=in_specs, out_specs=P("dp", "seq", None), check_vma=False
    )
```

time: 167 us -> 118 us (0.71)
  Pallas kernels: 0 us -> 99.9 us
  waiting for transfers between devices: 53.2 us -> 0 us
  blocking collectives: 33.6 us -> 0 us
  matrix products: 29.8 us -> 0 us
  local copies, waits for them, and re-layouts: 33.9 us -> 16.5 us
  other arithmetic: 8.02 us -> 0 us
  starting transfers between devices: 7.42 us -> 0 us
    pallas_call x0 -> x1, Pallas kernels: none -> 99.9 us  [on_device(): pl.pallas_call(functools.partial(kernel, groups, shards, rooms), out_shap...]
    all_to_all x1 -> x0, waiting for transfers between devices: 53.2 us -> none  [on_device(): lax.all_to_all(payload, 'dp', split_axis=0, concat_axis=0, tiled=True)]
    all_to_all x2 -> x0, blocking collectives: 33.6 us -> none  [the longest x1 16.8 us: on_device(): lax.all_to_all(selected, 'seq', split_axis=1, concat_axis=0, tiled=True)]
    dot_general x7 -> x0, matrix products: 22.9 us -> none  [the longest x2 6.24 us: attention(): jnp.einsum('bhqk,bkhs->bqhs', weights, parts[:, :, 2], preferred_element_...]
    unnamed x14 -> x4, local copies, waits for them, and re-layouts: 2.39 us -> 16.5 us
    all_to_all x1 -> x0, starting transfers between devices: 7.42 us -> none  [on_device(): lax.all_to_all(payload, 'dp', split_axis=0, concat_axis=0, tiled=True)]
    another operation x2 -> x0, local copies, waits for them, and re-layouts: 7.32 us -> none  [the longest x1 5.41 us: attention(): parts = qkv_rows.reshape(batch_count, length, 3, HEADS, HEAD_DIM)]
    sub x2 -> x0, matrix products: 6.89 us -> none  [attention(): raised = jnp.exp(scores - highest)]
  transfers between devices with their start and end apart: 1 -> 0, of which waited for: 1 -> 0; matrix products, arithmetic and copies ran while one was open for 0% -> 0% of each run, Pallas kernels for 0% -> 0%
where the time goes in v1:
time: 118 us; the launch traced here: 116 us
  Pallas kernels  99.9 us (85%)
  local copies, waits for them, and re-layouts  16.5 us (14%)
    pallas_call x1, Pallas kernels, on_device(): pl.pallas_call(functools.partial(kernel, groups, shards, rooms), out_shap...  99.9 us
    unnamed x4, local copies, waits for them, and re-layouts  16.5 us

profile of v1, /device:TPU:0, one launch (start us, length us, event | category | flops | bytes accessed | tf_op | source)
XLA Modules:
  0.0 116.5 jit_solution(3407011260313552850)
XLA Ops:
  0.0 1.4 %copy.13 = f32[1,6,1152]{2,1,0:T(8,128)} copy(f32[1,6,1152]{2,0,1:T(1,128)} %param.9) | data formatting | bytes 55296
  1.4 6.4 %copy.9.wqs_hbm = bf16[1152,1728]{1,0:T(8,128)(2,1)} copy(bf16[1152,1728]{0,1:T(8,128)(2,1)} %param.12) | data formatting | bytes 7962624 | tf_op args[4]
  7.8 6.5 %copy.10.wqt_hbm = bf16[1152,1728]{1,0:T(8,128)(2,1)} copy(bf16[1152,1728]{0,1:T(8,128)(2,1)} %param.14) | data formatting | bytes 7962624 | tf_op args[6]
  14.3 99.9 %shard_map.82 = bf16[7,4,16,1152]{3,2,1,0:T(8,128)(2,1)} custom-call(s32[8]{0:T(128)} %counts_ref.1, s32[8,13]{1,0:T(8,128)} %dest_ref.1, bf16[13,4,16,1152]{3,2,1,0:T(8,128)(2,1)} %bitcast.6, f32[6,1152]{1,0:T(8,128)} %bitcast.7, bf16[1152,1728]{1,0:T(8,128)(2,1)} %copy.9.wqs_hbm, bf16[576,1152]{1,0:T(8,128)(2,1)} %wos_hbm.1, ...), custom_call_target="tpu_custom_call" | custom-call | tf_op jit(solution)/shard_map/pallas_call | solution.py:257
  114.2 2.3 %copy.15 = bf16[7,64,1152]{2,1,0:T(8,128)(2,1)} copy(bf16[7,64,1152]{2,1,0:T(8,128)(2,1)} %bitcast.5) | data formatting | bytes 2064384

commit v2 on v1

v2 whole, which is shorter than its diff:
```python
import functools
import math

import jax
import jax.numpy as jnp
from jax import lax
from jax.experimental import pallas as pl
from jax.experimental.pallas import tpu as pltpu
from jax.sharding import PartitionSpec as P

HEADS = 8
HEAD_DIM = 72
NFD = 7
EPSILON = 1e-06
BATCH = 4
HALF = 8
MESH = pl.DeviceIdType.MESH


def norm_mod(values, shift_row, scale_row):
    center = values - jnp.mean(values, axis=-1, keepdims=True)
    spread = jnp.mean(center * center, axis=-1, keepdims=True)
    return (center * lax.rsqrt(spread + EPSILON) * (1.0 + scale_row) + shift_row).astype(jnp.bfloat16)


def flip(a, b, size):
    total, unit = 0, 1
    while unit < size:
        total = total + lax.rem(lax.rem(a // unit, 2) + lax.rem(b // unit, 2), 2) * unit
        unit *= 2
    return total


def project(rows, weight_t):
    return lax.dot_general(
        rows, weight_t[...], (((1,), (1,)), ((), ())), preferred_element_type=jnp.float32
    )


def attend(queries, qkv, same):
    width = HEADS * HEAD_DIM
    factor = 1.0 / math.sqrt(HEAD_DIM)
    mixed = []
    for head in range(HEADS):
        at = head * HEAD_DIM
        q = queries[:, at : at + HEAD_DIM]
        k = qkv[:, width + at : width + at + HEAD_DIM]
        v = qkv[:, 2 * width + at : 2 * width + at + HEAD_DIM]
        scores = lax.dot_general(q, k, (((1,), (1,)), ((), ())), preferred_element_type=jnp.float32)
        scores = jnp.where(same, scores * factor, -1e30)
        raised = jnp.exp(scores - jnp.max(scores, axis=-1, keepdims=True))
        weights = (raised * (1.0 / jnp.sum(raised, axis=-1, keepdims=True))).astype(jnp.bfloat16)
        mixed.append(jnp.dot(weights, v, preferred_element_type=jnp.float32))
    return jnp.concatenate(mixed, axis=-1)


def kernel(
    groups, shards, rooms,
    counts_ref, dest_ref, tok_ref, mod_ref, wqs_hbm, wos_hbm, wqt_hbm, wot_hbm,
    out_ref,
    wqs, wos, wqt, wot, send, arr, arr2, rows, res,
    w_sem, dp_send, dp_recv, sq_send, sq_recv, home_send, home_recv,
):
    group = lax.axis_index("dp")
    shard = lax.axis_index("seq")
    slots = tok_ref.shape[0]
    widest, width = tok_ref.shape[2], tok_ref.shape[3]
    patches = shards * widest
    room_slots = rooms * groups
    batches = room_slots // BATCH
    frames = NFD * shards

    barrier = pltpu.get_barrier_semaphore()

    def greet_dp(j, c):
        pl.semaphore_signal(
            barrier, inc=1, device_id=(flip(group, 1 + j, groups), shard), device_id_type=MESH
        )
        return c

    def greet_seq(i, c):
        pl.semaphore_signal(
            barrier, inc=1, device_id=(group, flip(shard, 1 + i, shards)), device_id_type=MESH
        )
        return c

    lax.fori_loop(0, groups - 1, greet_dp, 0)
    lax.fori_loop(0, shards - 1, greet_seq, 0)

    loads = [
        pltpu.make_async_copy(src, dst, w_sem.at[i])
        for i, (src, dst) in enumerate(
            ((wqs_hbm, wqs), (wos_hbm, wos), (wqt_hbm, wqt), (wot_hbm, wot))
        )
    ]
    for load in loads:
        load.start()

    held = counts_ref[group]

    def chosen(target, room):
        pick = jnp.int32(0)
        seen = jnp.int32(0)
        for q in range(slots):
            hit = jnp.logical_and(q < held, dest_ref[group, q] // NFD == target)
            pick = jnp.where(jnp.logical_and(hit, seen == room), jnp.int32(q), pick)
            seen = seen + hit.astype(jnp.int32)
        return pick

    def partner(i):
        near = lax.rem(i // 2 + 1, groups // 2)
        return flip(group, jnp.where(lax.rem(i, 2) == 0, groups // 2 + i // 2, near), groups)

    def dp_copy(t):
        target = partner(lax.rem(t, groups))
        return pltpu.make_async_remote_copy(
            src_ref=send.at[t], dst_ref=arr.at[t],
            send_sem=dp_send.at[t], recv_sem=dp_recv.at[t],
            device_id=(target, shard), device_id_type=MESH,
        )

    def pack(room):
        def body(j, c):
            t = room * groups + j
            send[t] = tok_ref[chosen(partner(j), room)]
            return c
        return body

    def start_dp(room):
        def body(j, c):
            dp_copy(room * groups + j).start()
            return c
        return body

    lax.fori_loop(0, groups, pack(0), 0)
    pl.semaphore_wait(barrier, groups + shards - 2)
    lax.fori_loop(0, groups - 1, start_dp(0), 0)
    for room in range(1, rooms):
        lax.fori_loop(0, groups, pack(room), 0)
        lax.fori_loop(0, groups - 1, start_dp(room), 0)
    for room in range(rooms):
        own = room * groups + groups - 1
        arr[own] = send[own]

    loads[0].wait()
    loads[1].wait()

    parts = [(b * BATCH, BATCH) for b in range(batches - 1)]
    parts += [((batches - 1) * BATCH + n * BATCH // 2, BATCH // 2) for n in range(2)]

    def seq_copy(b, first, size, x):
        peer = flip(shard, x, shards)
        return pltpu.make_async_remote_copy(
            src_ref=arr.at[pl.ds(first, size), peer],
            dst_ref=arr2.at[x, pl.ds(first, size)],
            send_sem=sq_send.at[b, x - 1], recv_sem=sq_recv.at[b, x - 1],
            device_id=(group, peer), device_id_type=MESH,
        )

    def same_frame(tall):
        frame_of = lax.broadcasted_iota(jnp.int32, (tall, tall), 0) // patches
        return frame_of == lax.broadcasted_iota(jnp.int32, (tall, tall), 1) // patches

    def spatial(b, first, size):
        tall = size * patches
        for n in range(size):
            t = first + n

            @pl.when(lax.rem(t, groups) != groups - 1)
            def _():
                dp_copy(t).wait_recv()

        x = arr[pl.ds(first, size)].astype(jnp.float32).reshape(tall, width)
        normed = norm_mod(x, mod_ref[0], mod_ref[1])
        qkv = project(normed, wqs).astype(jnp.bfloat16)
        mixed = attend(qkv, qkv, same_frame(tall)).astype(jnp.bfloat16)
        projected = jnp.dot(mixed, wos[...], preferred_element_type=jnp.float32)
        y = x + mod_ref[2] * projected
        arr[pl.ds(first, size)] = y.reshape(size, shards, widest, width).astype(jnp.bfloat16)
        for x in range(shards - 1, 0, -1):
            seq_copy(b, first, size, x).start()
        arr2[0, pl.ds(first, size)] = arr[pl.ds(first, size), shard]

    def full(b, c):
        spatial(b, b * BATCH, BATCH)
        return c

    lax.fori_loop(0, batches - 1, full, 0)
    short = BATCH // 2

    def last(n, c):
        spatial(batches - 1 + n, (batches - 1) * BATCH + n * short, short)
        return c

    lax.fori_loop(0, 2, last, 0)

    def find(source, found):
        found = list(found)
        live = counts_ref[source]
        seen = jnp.int32(0)
        apart = flip(source, group, groups)
        near = 2 * lax.rem(apart + groups // 2 - 1, groups // 2) + 1
        offset = jnp.where(apart >= groups // 2, 2 * (apart - groups // 2), near)
        for q in range(slots):
            place = dest_ref[source, q] - group * NFD
            hit = jnp.logical_and(q < live, jnp.logical_and(place >= 0, place < NFD))
            code = seen * groups + offset
            for k in range(NFD):
                found[k] = jnp.where(jnp.logical_and(hit, place == k), code, found[k])
            seen = seen + hit.astype(jnp.int32)
        return tuple(found)

    found = lax.fori_loop(0, groups, find, (jnp.int32(0),) * NFD)

    loads[2].wait()
    loads[3].wait()

    for b, (first, size) in enumerate(parts):
        for x in range(1, shards):
            seq_copy(b, first, size, x).wait_recv()

    order = list(range(shards - 1, -1, -1))
    for place, x in enumerate(order):
        for k in range(NFD):
            rows[place * NFD + k] = arr2[x, found[k]]

    def home_copy(x):
        peer = flip(shard, x, shards)
        return pltpu.make_async_remote_copy(
            src_ref=res.at[x], dst_ref=out_ref.at[:, shard],
            send_sem=home_send.at[x - 1], recv_sem=home_recv.at[x - 1],
            device_id=(group, peer), device_id_type=MESH,
        )

    halves = widest // HALF
    pieces = 2
    some = frames // pieces
    part = frames * HALF
    tokens = rows[...].astype(jnp.float32).reshape(frames * widest, width)
    normed = norm_mod(tokens, mod_ref[3], mod_ref[4])
    qkv = project(normed, wqt).reshape(frames, widest, 3 * HEADS * HEAD_DIM)
    by_patch = [
        qkv[:, n * HALF : (n + 1) * HALF, :].reshape(part, qkv.shape[-1]).astype(jnp.bfloat16)
        for n in range(halves)
    ]
    patch_of = lax.rem(lax.broadcasted_iota(jnp.int32, (some * HALF, part), 0), HALF)
    same_patch = patch_of == lax.rem(
        lax.broadcasted_iota(jnp.int32, (some * HALF, part), 1), HALF
    )
    for piece in range(pieces):
        begin = piece * some
        mixed = [
            attend(rows_of[begin * HALF : (begin + some) * HALF], rows_of, same_patch).reshape(
                some, HALF, HEADS * HEAD_DIM
            )
            for rows_of in by_patch
        ]
        mixed = jnp.concatenate(mixed, axis=1).reshape(some * widest, HEADS * HEAD_DIM)
        projected = jnp.dot(mixed.astype(jnp.bfloat16), wot[...], preferred_element_type=jnp.float32)
        y = rows[pl.ds(begin, some)].astype(jnp.float32) + (mod_ref[5] * projected).reshape(
            some, widest, width
        )
        y = y.astype(jnp.bfloat16).reshape(shards // pieces, NFD, widest, width)
        for n in range(shards // pieces):
            x = order[piece * shards // pieces + n]
            if x:
                res[x] = y[n]
                home_copy(x).start()
            else:
                out_ref[:, shard] = y[n]

    for room in range(rooms):
        def sent(j, c):
            dp_copy(room * groups + j).wait_send()
            return c
        lax.fori_loop(0, groups - 1, sent, 0)

    for b, (first, size) in enumerate(parts):
        for x in range(1, shards):
            seq_copy(b, first, size, x).wait_send()
    for x in range(1, shards):
        home_copy(x).wait()


def solution(mesh):
    groups, shards = mesh.shape["dp"], mesh.shape["seq"]

    def on_device(tokens, modulation, counts, dest, wqs, wos, wqt, wot):
        slots, patches, width = tokens.shape
        rooms = (slots + groups - 1) // groups
        widest = patches // shards
        total = rooms * groups
        bf = jnp.bfloat16
        vmem = pl.BlockSpec(memory_space=pltpu.VMEM)
        smem = pl.BlockSpec(memory_space=pltpu.SMEM)
        hbm = pl.BlockSpec(memory_space=pl.ANY)
        dma = pltpu.SemaphoreType.DMA
        out = pl.pallas_call(
            functools.partial(kernel, groups, shards, rooms),
            out_shape=jax.ShapeDtypeStruct((NFD, shards, widest, width), bf),
            in_specs=[smem, smem, vmem, vmem, hbm, hbm, hbm, hbm],
            out_specs=vmem,
            scratch_shapes=[
                pltpu.VMEM(wqs.shape[::-1], bf),
                pltpu.VMEM(wos.shape, bf),
                pltpu.VMEM(wqt.shape[::-1], bf),
                pltpu.VMEM(wot.shape, bf),
                pltpu.VMEM((total, shards, widest, width), bf),
                pltpu.VMEM((total, shards, widest, width), bf),
                pltpu.VMEM((shards, total, widest, width), bf),
                pltpu.VMEM((NFD * shards, widest, width), bf),
                pltpu.VMEM((shards, NFD, widest, width), bf),
                dma((4,)),
                dma((total,)),
                dma((total,)),
                dma((total // BATCH + 1, shards - 1)),
                dma((total // BATCH + 1, shards - 1)),
                dma((shards - 1,)),
                dma((shards - 1,)),
            ],
            compiler_params=pltpu.CompilerParams(
                collective_id=0, has_side_effects=True, vmem_limit_bytes=60 * 1024 * 1024
            ),
        )(
            counts, dest, tokens.reshape(slots, shards, widest, width),
            modulation.transpose(1, 0, 2), wqs.T, wos, wqt.T, wot,
        )
        return out.reshape(NFD, patches, width)

    in_specs = (P("dp", "seq", None), P("dp", None, None), P(), P(), P(), P(), P(), P())
    return jax.shard_map(
        on_device, mesh=mesh, in_specs=in_specs, out_specs=P("dp", "seq", None), check_vma=False
    )
```

time: 118 us -> 97 us (0.82); the launches traced: 116 us -> 96.8 us
  local copies, waits for them, and re-layouts: 16.5 us -> 2.26 us
  Pallas kernels: 99.9 us -> 94.6 us
    unnamed x4 -> x1, local copies, waits for them, and re-layouts: 16.5 us -> 2.26 us
    pallas_call x1, Pallas kernels: 99.9 us -> 94.6 us  [on_device(): pl.pallas_call(functools.partial(kernel, groups, shards, rooms), out_shap...]
where the time goes in v2:
time: 97 us; the launch traced here: 96.8 us
  Pallas kernels  94.6 us (98%)
  local copies, waits for them, and re-layouts  2.26 us (2%)
    pallas_call x1, Pallas kernels, on_device(): pl.pallas_call(functools.partial(kernel, groups, shards, rooms), out_shap...  94.6 us
    unnamed x1, local copies, waits for them, and re-layouts  2.26 us

profile of v2, /device:TPU:0, one launch (start us, length us, event | category | flops | bytes accessed | tf_op | source)
XLA Modules:
  0.0 96.8 jit_solution(16064527689310834264)
XLA Ops:
  0.0 94.6 %shard_map.82 = bf16[7,4,16,1152]{3,2,1,0:T(8,128)(2,1)} custom-call(s32[8]{0:T(128)} %counts_ref.1, s32[8,13]{1,0:T(8,128)} %dest_ref.1, bf16[13,4,16,1152]{3,2,1,0:T(8,128)(2,1)} %bitcast.8, f32[6,1,1152]{2,1,0:T(1,128)} %bitcast.9, bf16[1728,1152]{1,0:T(8,128)(2,1)} %bitcast.6, bf16[576,1152]{1,0:T(8,128)(2,1)} %wos_hbm.1, bf16[1728,1152]{1,0:T(8,128)(2,1)} %bitcast.7, ...), custom_call_target="tpu_custom_call" | custom-call | tf_op jit(solution)/shard_map/pallas_call | solution.py:298
  94.6 2.3 %copy.10 = bf16[7,64,1152]{2,1,0:T(8,128)(2,1)} copy(bf16[7,64,1152]{2,1,0:T(8,128)(2,1)} %bitcast.5) | data formatting | bytes 2064384

commit v3 on v2

--- a/solution.py
+++ b/solution.py
@@ -55,10 +55,10 @@
 
 
 def kernel(
-    groups, shards, rooms,
+    groups, shards, rooms, extra_count,
     counts_ref, dest_ref, tok_ref, mod_ref, wqs_hbm, wos_hbm, wqt_hbm, wot_hbm,
     out_ref,
-    wqs, wos, wqt, wot, send, arr, arr2, rows, res,
+    wqs, wos, wqt, wot, send, arr, over, arr2, qkv2, rows, qkv_rows, res,
     w_sem, dp_send, dp_recv, sq_send, sq_recv, home_send, home_recv,
 ):
     group = lax.axis_index("dp")
@@ -66,8 +66,7 @@
     slots = tok_ref.shape[0]
     widest, width = tok_ref.shape[2], tok_ref.shape[3]
     patches = shards * widest
-    room_slots = rooms * groups
-    batches = room_slots // BATCH
+    batches = groups // BATCH
     frames = NFD * shards
 
     barrier = pltpu.get_barrier_semaphore()
@@ -145,13 +144,14 @@
     loads[0].wait()
     loads[1].wait()
 
-    parts = [(b * BATCH, BATCH) for b in range(batches - 1)]
-    parts += [((batches - 1) * BATCH + n * BATCH // 2, BATCH // 2) for n in range(2)]
-
-    def seq_copy(b, first, size, x):
+    parts = [(b * BATCH, BATCH) for b in range(batches)]
+    if extra_count:
+        parts.append((groups, extra_count))
+
+    def seq_copy(b, src, first, size, x):
         peer = flip(shard, x, shards)
         return pltpu.make_async_remote_copy(
-            src_ref=arr.at[pl.ds(first, size), peer],
+            src_ref=src.at[:, peer] if src is over else src.at[pl.ds(first, size), peer],
             dst_ref=arr2.at[x, pl.ds(first, size)],
             send_sem=sq_send.at[b, x - 1], recv_sem=sq_recv.at[b, x - 1],
             device_id=(group, peer), device_id_type=MESH,
@@ -161,41 +161,53 @@
         frame_of = lax.broadcasted_iota(jnp.int32, (tall, tall), 0) // patches
         return frame_of == lax.broadcasted_iota(jnp.int32, (tall, tall), 1) // patches
 
-    def spatial(b, first, size):
+    def spatial(values, size):
         tall = size * patches
-        for n in range(size):
-            t = first + n
-
-            @pl.when(lax.rem(t, groups) != groups - 1)
-            def _():
-                dp_copy(t).wait_recv()
-
-        x = arr[pl.ds(first, size)].astype(jnp.float32).reshape(tall, width)
-        normed = norm_mod(x, mod_ref[0], mod_ref[1])
+        tokens = values.astype(jnp.float32).reshape(tall, width)
+        normed = norm_mod(tokens, mod_ref[0], mod_ref[1])
         qkv = project(normed, wqs).astype(jnp.bfloat16)
         mixed = attend(qkv, qkv, same_frame(tall)).astype(jnp.bfloat16)
         projected = jnp.dot(mixed, wos[...], preferred_element_type=jnp.float32)
-        y = x + mod_ref[2] * projected
-        arr[pl.ds(first, size)] = y.reshape(size, shards, widest, width).astype(jnp.bfloat16)
+        y = tokens + mod_ref[2] * projected
+        return y.reshape(size, shards, widest, width).astype(jnp.bfloat16)
+
+    def full(b, c):
+        for n in range(BATCH):
+            t = b * BATCH + n
+
+            @pl.when(t != groups - 1)
+            def _():
+                dp_copy(t).wait_recv()
+
+        at = pl.ds(b * BATCH, BATCH)
+        arr[at] = spatial(arr[at], BATCH)
         for x in range(shards - 1, 0, -1):
-            seq_copy(b, first, size, x).start()
-        arr2[0, pl.ds(first, size)] = arr[pl.ds(first, size), shard]
-
-    def full(b, c):
-        spatial(b, b * BATCH, BATCH)
+            seq_copy(b, arr, b * BATCH, BATCH, x).start()
+        arr2[0, at] = arr[at, shard]
         return c
 
-    lax.fori_loop(0, batches - 1, full, 0)
-    short = BATCH // 2
-
-    def last(n, c):
-        spatial(batches - 1 + n, (batches - 1) * BATCH + n * short, short)
+    lax.fori_loop(0, batches, full, 0)
+
+    loads[2].wait()
+    loads[3].wait()
+
+    def prepare(b, src, first, size):
+        for x in range(1, shards):
+            seq_copy(b, src, first, size, x).wait_recv()
+        tokens = arr2[:, pl.ds(first, size)].astype(jnp.float32).reshape(-1, width)
+        qkv = project(norm_mod(tokens, mod_ref[3], mod_ref[4]), wqt)
+        qkv2[:, pl.ds(first, size)] = qkv.reshape(
+            shards, size, widest, qkv.shape[-1]
+        ).astype(jnp.bfloat16)
+
+    def prepare_full(b, c):
+        prepare(b, arr, b * BATCH, BATCH)
         return c
 
-    lax.fori_loop(0, 2, last, 0)
-
-    def find(source, found):
-        found = list(found)
+    lax.fori_loop(0, batches, prepare_full, 0)
+
+    def find(source, state):
+        found, extra, taken = list(state[0]), list(state[1]), state[2]
         live = counts_ref[source]
         seen = jnp.int32(0)
         apart = flip(source, group, groups)
@@ -204,25 +216,42 @@
         for q in range(slots):
             place = dest_ref[source, q] - group * NFD
             hit = jnp.logical_and(q < live, jnp.logical_and(place >= 0, place < NFD))
-            code = seen * groups + offset
+            second = jnp.logical_and(hit, seen >= 1)
+            code = jnp.where(second, groups + taken, offset)
             for k in range(NFD):
                 found[k] = jnp.where(jnp.logical_and(hit, place == k), code, found[k])
+            for e in range(extra_count):
+                extra[e] = jnp.where(
+                    jnp.logical_and(second, taken == e), seen * groups + offset, extra[e]
+                )
+            taken = taken + second.astype(jnp.int32)
             seen = seen + hit.astype(jnp.int32)
-        return tuple(found)
-
-    found = lax.fori_loop(0, groups, find, (jnp.int32(0),) * NFD)
-
-    loads[2].wait()
-    loads[3].wait()
-
-    for b, (first, size) in enumerate(parts):
-        for x in range(1, shards):
-            seq_copy(b, first, size, x).wait_recv()
+        return tuple(found), tuple(extra), taken
+
+    zero = jnp.int32(0)
+    found, extra, _ = lax.fori_loop(
+        0, groups, find, ((zero,) * NFD, (zero,) * extra_count, zero)
+    )
+
+    if extra_count:
+        for room in range(1, rooms):
+            def come(j, c):
+                dp_copy(room * groups + j).wait_recv()
+                return c
+            lax.fori_loop(0, groups - 1, come, 0)
+        for e in range(extra_count):
+            over[e] = arr[extra[e]]
+        over[...] = spatial(over[...], extra_count)
+        for x in range(shards - 1, 0, -1):
+            seq_copy(batches, over, groups, extra_count, x).start()
+        arr2[0, pl.ds(groups, extra_count)] = over[:, shard]
+        prepare(batches, over, groups, extra_count)
 
     order = list(range(shards - 1, -1, -1))
     for place, x in enumerate(order):
         for k in range(NFD):
             rows[place * NFD + k] = arr2[x, found[k]]
+            qkv_rows[place * NFD + k] = qkv2[x, found[k]]
 
     def home_copy(x):
         peer = flip(shard, x, shards)
@@ -236,9 +265,7 @@
     pieces = 2
     some = frames // pieces
     part = frames * HALF
-    tokens = rows[...].astype(jnp.float32).reshape(frames * widest, width)
-    normed = norm_mod(tokens, mod_ref[3], mod_ref[4])
-    qkv = project(normed, wqt).reshape(frames, widest, 3 * HEADS * HEAD_DIM)
+    qkv = qkv_rows[...].astype(jnp.float32)
     by_patch = [
         qkv[:, n * HALF : (n + 1) * HALF, :].reshape(part, qkv.shape[-1]).astype(jnp.bfloat16)
         for n in range(halves)
@@ -277,7 +304,7 @@
 
     for b, (first, size) in enumerate(parts):
         for x in range(1, shards):
-            seq_copy(b, first, size, x).wait_send()
+            seq_copy(b, over if first == groups else arr, first, size, x).wait_send()
     for x in range(1, shards):
         home_copy(x).wait()
 
@@ -290,13 +317,15 @@
         rooms = (slots + groups - 1) // groups
         widest = patches // shards
         total = rooms * groups
+        extras = NFD * (rooms - 1) // rooms
+        kinds = wqs.shape[-1]
         bf = jnp.bfloat16
         vmem = pl.BlockSpec(memory_space=pltpu.VMEM)
         smem = pl.BlockSpec(memory_space=pltpu.SMEM)
         hbm = pl.BlockSpec(memory_space=pl.ANY)
         dma = pltpu.SemaphoreType.DMA
         out = pl.pallas_call(
-            functools.partial(kernel, groups, shards, rooms),
+            functools.partial(kernel, groups, shards, rooms, extras),
             out_shape=jax.ShapeDtypeStruct((NFD, shards, widest, width), bf),
             in_specs=[smem, smem, vmem, vmem, hbm, hbm, hbm, hbm],
             out_specs=vmem,
@@ -307,14 +336,17 @@
                 pltpu.VMEM(wot.shape, bf),
                 pltpu.VMEM((total, shards, widest, width), bf),
                 pltpu.VMEM((total, shards, widest, width), bf),
-                pltpu.VMEM((shards, total, widest, width), bf),
+                pltpu.VMEM((max(extras, 1), shards, widest, width), bf),
+                pltpu.VMEM((shards, groups + extras, widest, width), bf),
+                pltpu.VMEM((shards, groups + extras, widest, kinds), bf),
                 pltpu.VMEM((NFD * shards, widest, width), bf),
+                pltpu.VMEM((NFD * shards, widest, kinds), bf),
                 pltpu.VMEM((shards, NFD, widest, width), bf),
                 dma((4,)),
                 dma((total,)),
                 dma((total,)),
-                dma((total // BATCH + 1, shards - 1)),
-                dma((total // BATCH + 1, shards - 1)),
+                dma((groups // BATCH + 1, shards - 1)),
+                dma((groups // BATCH + 1, shards - 1)),
                 dma((shards - 1,)),
                 dma((shards - 1,)),
             ],

time: 97 us -> 92.9 us (0.958)
  the two profiles are of different devices: /device:TPU:0 before, /device:TPU:12 now
where the time goes in v3:
time: 92.9 us; the launch traced here: 92.7 us
  Pallas kernels  90.4 us (97%)
  local copies, waits for them, and re-layouts  2.26 us (2%)
    pallas_call x1, Pallas kernels, on_device(): pl.pallas_call(functools.partial(kernel, groups, shards, rooms, extras),...  90.4 us
    unnamed x1, local copies, waits for them, and re-layouts  2.26 us

profile of v3, /device:TPU:12, one launch (start us, length us, event | category | flops | bytes accessed | tf_op | source)
XLA Modules:
  0.0 92.7 jit_solution(14531355528367522957)
XLA Ops:
  0.0 90.4 %shard_map.82 = bf16[7,4,16,1152]{3,2,1,0:T(8,128)(2,1)} custom-call(s32[8]{0:T(128)} %counts_ref.1, s32[8,13]{1,0:T(8,128)} %dest_ref.1, bf16[13,4,16,1152]{3,2,1,0:T(8,128)(2,1)} %bitcast.8, f32[6,1,1152]{2,1,0:T(1,128)} %bitcast.9, bf16[1728,1152]{1,0:T(8,128)(2,1)} %bitcast.6, bf16[576,1152]{1,0:T(8,128)(2,1)} %wos_hbm.1, bf16[1728,1152]{1,0:T(8,128)(2,1)} %bitcast.7, ...), custom_call_target="tpu_custom_call" | custom-call | tf_op jit(solution)/shard_map/pallas_call | solution.py:327
  90.4 2.3 %copy.10 = bf16[7,64,1152]{2,1,0:T(8,128)(2,1)} copy(bf16[7,64,1152]{2,1,0:T(8,128)(2,1)} %bitcast.5) | data formatting | bytes 2064384

commit v4 on v3

--- a/solution.py
+++ b/solution.py
@@ -136,7 +136,6 @@
     lax.fori_loop(0, groups - 1, start_dp(0), 0)
     for room in range(1, rooms):
         lax.fori_loop(0, groups, pack(room), 0)
-        lax.fori_loop(0, groups - 1, start_dp(room), 0)
     for room in range(rooms):
         own = room * groups + groups - 1
         arr[own] = send[own]
@@ -178,6 +177,14 @@
             @pl.when(t != groups - 1)
             def _():
                 dp_copy(t).wait_recv()
+
+        for n in range(BATCH):
+            t = b * BATCH + n
+
+            @pl.when(t != groups - 1)
+            def _():
+                for room in range(1, rooms):
+                    dp_copy(room * groups + t).start()
 
         at = pl.ds(b * BATCH, BATCH)
         arr[at] = spatial(arr[at], BATCH)

time: 92.9 us -> 93.6 us (level)
  no operation moved by 1% of the time
where the time goes in v4:
time: 93.6 us; the launch traced here: 93.4 us
  Pallas kernels  91.1 us (97%)
  local copies, waits for them, and re-layouts  2.26 us (2%)
    pallas_call x1, Pallas kernels, on_device(): pl.pallas_call(functools.partial(kernel, groups, shards, rooms, extras),...  91.1 us
    unnamed x1, local copies, waits for them, and re-layouts  2.26 us

profile of v4, /device:TPU:12, one launch (start us, length us, event | category | flops | bytes accessed | tf_op | source)
XLA Modules:
  0.0 93.4 jit_solution(13544580020883365562)
XLA Ops:
  0.0 91.1 %shard_map.82 = bf16[7,4,16,1152]{3,2,1,0:T(8,128)(2,1)} custom-call(s32[8]{0:T(128)} %counts_ref.1, s32[8,13]{1,0:T(8,128)} %dest_ref.1, bf16[13,4,16,1152]{3,2,1,0:T(8,128)(2,1)} %bitcast.8, f32[6,1,1152]{2,1,0:T(1,128)} %bitcast.9, bf16[1728,1152]{1,0:T(8,128)(2,1)} %bitcast.6, bf16[576,1152]{1,0:T(8,128)(2,1)} %wos_hbm.1, bf16[1728,1152]{1,0:T(8,128)(2,1)} %bitcast.7, ...), custom_call_target="tpu_custom_call" | custom-call | tf_op jit(solution)/shard_map/pallas_call | solution.py:334
  91.1 2.3 %copy.10 = bf16[7,64,1152]{2,1,0:T(8,128)(2,1)} copy(bf16[7,64,1152]{2,1,0:T(8,128)(2,1)} %bitcast.5) | data formatting | bytes 2064384
